TPU v7x, 256 devices: a whole 4x4x8 slice. The times are simulated.
256 devices in a mesh: depth: 16 (over z, core), image: 16 (over x, y).
Axes of the slice: x: 4, y: 4, z: 8, core: 2. Of those that a mesh axis runs over, the one named last changes fastest.
Arguments:
- level_set: float32 [256, 1024, 512], P('depth', 'image'), may hold values from -6 to 6
- velocity: float32 [3, 256, 1024, 512], P(None, 'depth', 'image'), may hold values from -1 to 1
- view_flag: int32 [16], replicated, may hold values from 0 to 1
- slab_rank: int32 [16], replicated, may hold values from 0 to 15, each once
Outputs:
- image_first: float32 [4, 1024, 512], P(None, 'image', 'depth')
- image_second: float32 [4, 1024, 512], P(None, 'image', 'depth')
- level_next: float32 [256, 1024, 512], P('depth', 'image')
Inputs may be any that keep to these rules, and one draw needn't show every extreme that they name: `slab_rank`: each of 0 to 15 once.
All inputs are finite; a program needn't handle non-finite values.
Results may differ from a plain program's by a relative error of at most 0.00013.
Values sent between devices are 32-bit elements; how exact they have to be, the bound alone decides.
A program may use at most 64 MiB of HBM per device.

v0:
```python
import jax
import jax.numpy as jnp
from jax import lax
from jax.sharding import PartitionSpec as P

STEPS = 4


step_size = 0.3


def padded_2(array, sides, width):
    edges = {}
    for axis, dim in sides:
        size, length = (lax.axis_size(axis), array.shape[dim])
        up = [(i, (i + 1) % size) for i in range(size - 1)]
        last = lax.slice_in_dim(array, length - width, length, axis=dim)
        leading = lax.slice_in_dim(array, 0, width, axis=dim)
        edges[dim] = (
            lax.ppermute(last, axis, up),
            lax.ppermute(leading, axis, [(b, a) for a, b in up]),
        )
    done = []
    for _, dim in sides:
        low, high = edges[dim]
        around = [(width, width) if d in done else (0, 0) for d in range(array.ndim)]
        array = jnp.concatenate([jnp.pad(low, around), array, jnp.pad(high, around)], axis=dim)
        done.append(dim)
    return array


def update(padded, velocity):
    center = padded[1:-1, 1:-1, 1:-1]
    lows = (padded[:-2, 1:-1, 1:-1], padded[1:-1, :-2, 1:-1], padded[1:-1, 1:-1, :-2])
    highs = (padded[2:, 1:-1, 1:-1], padded[1:-1, 2:, 1:-1], padded[1:-1, 1:-1, 2:])
    rate = jnp.zeros_like(center)
    for k in range(3):
        speed = velocity[k]
        rate = (
            rate
            + jnp.maximum(speed, 0.0) * (center - lows[k])
            + jnp.minimum(speed, 0.0) * (highs[k] - center)
        )
    return center - step_size * rate


def advect_single(field, velocity):
    padded = padded_2(field, (("depth", 0), ("image", 1)), 1)
    padded = jnp.pad(padded, ((0, 0), (0, 0), (1, 1)))
    return update(padded, velocity)


def render_brick(field, flag, scale):
    density = scale * jnp.exp(-field * field)
    colour = jnp.stack(
        [jax.nn.sigmoid(2.0 * field), jnp.exp(-field * field), jax.nn.sigmoid(-2.0 * field)], axis=0
    )
    running = jnp.cumsum(density, axis=0)
    totals = running[-1:]
    before = jnp.where(flag[0] == 0, running - density, totals - running)
    weight = jnp.exp(-before) * (1.0 - jnp.exp(-density))
    partial_colour = jnp.sum(weight[None] * colour, axis=1)
    return (partial_colour, -totals[0])


def composite(frames, slab_rank):
    count = len(frames)
    depth_count = lax.axis_size("depth")
    colours = jnp.stack([frame[0] for frame in frames], axis=0)
    logs = jnp.stack([frame[1] for frame in frames], axis=0)
    rows, cols = (logs.shape[1], logs.shape[2])
    width = cols // depth_count
    packed = jnp.concatenate([colours, logs[:, None]], axis=1)
    received = lax.all_to_all(packed, "depth", split_axis=3, concat_axis=0, tiled=True)
    received = received.reshape(depth_count, count, 4, rows, width)
    earlier_mask = (slab_rank[None, :] < slab_rank[:, None]).astype(jnp.float32)
    log_parts = received[:, :, 3]
    earlier = jnp.einsum("de,efxy->dfxy", earlier_mask, log_parts, precision=lax.Precision.HIGHEST)
    rgb = jnp.sum(jnp.exp(earlier)[:, :, None] * received[:, :, :3], axis=0)
    alpha = 1.0 - jnp.exp(jnp.sum(log_parts, axis=0))
    result = jnp.concatenate([rgb, alpha[:, None]], axis=1)
    return [result[0]]


def local(level_set, velocity, view_flag, slab_rank):
    scale = 2.0 / (level_set.shape[0] * lax.axis_size("depth"))
    own_flag = lax.dynamic_slice_in_dim(view_flag, lax.axis_index("depth"), 1)
    first = render_brick(level_set, own_flag, scale)
    field = level_set
    for step in range(STEPS):
        field = advect_single(field, velocity)
    second = render_brick(field, own_flag, scale)
    image_first = composite([first], slab_rank)[0]
    image_second = composite([second], slab_rank)[0]
    return (image_first, image_second, field)


def solution(mesh):
    placed = (P("depth", "image", None), P(None, "depth", "image", None), P(), P())
    return jax.shard_map(
        local,
        mesh=mesh,
        in_specs=placed,
        out_specs=(P(None, "image", "depth"), P(None, "image", "depth"), P("depth", "image", None)),
        check_vma=False,
    )
```

profile of v0, /device:TPU:27, one launch (start us, length us, event | category | flops | bytes accessed | tf_op | source)
XLA Modules:
  0.0 151.2 jit_solution(3199686916753563401)
XLA Ops:
  1.7 2.4 %collective-permute-start.3 = (f32[16,1,512]{2,1,0:T(1,128)S(1)}, f32[16,1,512]{2,1,0:T(1,128)S(1)}, u32[]{:S(2)}, u32[]{:S(2)}) collective-permute-start(f32[16,1,512]{2,1,0:T(1,128)S(1)} %get-tuple-element.28), channel_id=1, source_target_pairs={{1,0},{2,1},{3,2},{4,3},{5,4},{6,5},{7,6},{8,7},{9,8},{10,9},{11,1... | collective-permute-start | bytes 98312 | tf_op jit(solution)/shard_map/ppermute | solution.py:21
  5.1 4.4 %collective-permute-start = (f32[1,64,512]{2,1,0:T(8,128)S(1)}, f32[1,64,512]{2,1,0:T(8,128)S(1)}, u32[]{:S(2)}, u32[]{:S(2)}) collective-permute-start(f32[1,64,512]{2,1,0:T(8,128)S(1)} %get-tuple-element.30), channel_id=1, source_target_pairs={{0,16},{16,32},{32,48},{48,64},{64,80},{80,96},{96,112},{112,128},... | collective-permute-start | bytes 393224 | tf_op jit(solution)/shard_map/ppermute | solution.py:20
  9.5 1.9 %collective-permute-start.1 = (f32[1,64,512]{2,1,0:T(8,128)S(1)}, f32[1,64,512]{2,1,0:T(8,128)S(1)}, u32[]{:S(2)}, u32[]{:S(2)}) collective-permute-start(f32[1,64,512]{2,1,0:T(8,128)S(1)} %get-tuple-element.29), channel_id=1, source_target_pairs={{16,0},{32,16},{48,32},{64,48},{80,64},{96,80},{112,96},{128,112},... | collective-permute-start | bytes 393224 | tf_op jit(solution)/shard_map/ppermute | solution.py:21
  11.4 5.0 %collective-permute-start.2 = (f32[16,1,512]{2,1,0:T(1,128)S(1)}, f32[16,1,512]{2,1,0:T(1,128)S(1)}, u32[]{:S(2)}, u32[]{:S(2)}) collective-permute-start(f32[16,1,512]{2,1,0:T(1,128)S(1)} %get-tuple-element.27), channel_id=1, source_target_pairs={{0,1},{1,2},{2,3},{3,4},{4,5},{5,6},{6,7},{7,8},{8,9},{9,10},{10,1... | collective-permute-start | bytes 98312 | tf_op jit(solution)/shard_map/ppermute | solution.py:20
  16.5 2.2 %fusion.75 = f32[16,64,512]{2,1,0:T(8,128)S(1)} fusion(f32[16,64,512]{2,1,0:T(8,128)} %param.4), kind=kOutput, calls=%fused_computation.143 | output fusion | flops 9437184 | bytes 4194304 | tf_op jit(solution)/shard_map/jit(cumsum)/reduce_window_sum | solution.py:58
  21.4 1.9 %constant_dynamic-update-slice_fusion.1 = f32[18,64,512]{2,1,0:T(8,128)S(1)} fusion(f32[18,64,512]{2,1,0:T(8,128)S(1)} %constant_dynamic-update-slice_fusion.2, f32[16,64,512]{2,1,0:T(8,128)} %param.4), kind=kLoop, calls=%fused_computation.174 | loop fusion | bytes 4194304
  25.7 6.7 %fusion.59 = (f32[16,64,512]{2,1,0:T(8,128)S(1)}, f32[1,16,64,512]{3,2,1,0:T(8,128)}, f32[16,64,512]{2,1,0:T(8,128)}, f32[1,16,64,512]{3,2,1,0:T(8,128)}, f32[1,16,64,512]{3,2,1,0:T(8,128)}) fusion(f32[16,64,512]{2,1,0:T(8,128)S(1)} %copy-done, f32[18,66,514]{2,1,0:T(8,128)S(1)} %select_maximum_fusion.12, f32[18,1,512]{2,1,0:T(1,128)S(1)} %pad.39, ...), kind=kLoop, calls=%fused_computation.110 | loop fusion | flops 24641536 | bytes 27992064 | tf_op jit(solution)/shard_map/sub | solution.py:44
  32.4 1.9 %collective-permute-start.5 = (f32[1,64,512]{2,1,0:T(8,128)S(1)}, f32[1,64,512]{2,1,0:T(8,128)S(1)}, u32[]{:S(2)}, u32[]{:S(2)}) collective-permute-start(f32[1,64,512]{2,1,0:T(8,128)S(1)} %get-tuple-element.19), channel_id=1, source_target_pairs={{16,0},{32,16},{48,32},{64,48},{80,64},{96,80},{112,96},{128,112},... | collective-permute-start | bytes 393224 | tf_op jit(solution)/shard_map/ppermute | solution.py:21
  34.4 3.9 %collective-permute-start.4 = (f32[1,64,512]{2,1,0:T(8,128)S(1)}, f32[1,64,512]{2,1,0:T(8,128)S(1)}, u32[]{:S(2)}, u32[]{:S(2)}) collective-permute-start(f32[1,64,512]{2,1,0:T(8,128)S(1)} %get-tuple-element.18), channel_id=1, source_target_pairs={{0,16},{16,32},{32,48},{48,64},{64,80},{80,96},{96,112},{112,128},... | collective-permute-start | bytes 393224 | tf_op jit(solution)/shard_map/ppermute | solution.py:20
  38.4 1.9 %collective-permute-start.7 = (f32[16,1,512]{2,1,0:T(1,128)S(1)}, f32[16,1,512]{2,1,0:T(1,128)S(1)}, u32[]{:S(2)}, u32[]{:S(2)}) collective-permute-start(f32[16,1,512]{2,1,0:T(1,128)S(1)} %get-tuple-element.21), channel_id=1, source_target_pairs={{1,0},{2,1},{3,2},{4,3},{5,4},{6,5},{7,6},{8,7},{9,8},{10,9},{11,1... | collective-permute-start | bytes 98312 | tf_op jit(solution)/shard_map/ppermute | solution.py:21
  40.3 5.5 %collective-permute-start.6 = (f32[16,1,512]{2,1,0:T(1,128)S(1)}, f32[16,1,512]{2,1,0:T(1,128)S(1)}, u32[]{:S(2)}, u32[]{:S(2)}) collective-permute-start(f32[16,1,512]{2,1,0:T(1,128)S(1)} %get-tuple-element.20), channel_id=1, source_target_pairs={{0,1},{1,2},{2,3},{3,4},{4,5},{5,6},{6,7},{7,8},{8,9},{9,10},{10,1... | collective-permute-start | bytes 98312 | tf_op jit(solution)/shard_map/ppermute | solution.py:20
  46.8 3.0 %select_maximum_fusion.8 = f32[18,66,514]{2,1,0:T(8,128)S(1)} fusion(f32[18,1,512]{2,1,0:T(1,128)S(1)} %pad.42, f32[18,1,512]{2,1,0:T(1,128)S(1)} %pad.41, f32[1,64,512]{2,1,0:T(8,128)S(1)} %collective-permute-done.5, f32[16,64,512]{2,1,0:T(8,128)S(1)} %get-tuple-element.22, f32[1,64,512]{2,1,0:T(8,128)S(1)} %collective-permute-done.4), kind=kLoop, calls=%fused_computation.14 | loop fusion | flops 7327584 | bytes 4875552 | tf_op jit(solution)/shard_map/concatenate | solution.py:27
  49.9 3.5 %fusion.42 = f32[16,64,512]{2,1,0:T(8,128)S(1)} fusion(f32[16,64,512]{2,1,0:T(8,128)S(1)} %get-tuple-element.22, f32[18,66,514]{2,1,0:T(8,128)S(1)} %select_maximum_fusion.8, f32[18,1,512]{2,1,0:T(1,128)S(1)} %pad.42, f32[1,64,512]{2,1,0:T(8,128)S(1)} %collective-permute-done.5, f32[1,64,512]{2,1,0:T(8,128)S(1)} %collective-permute-done.4, ...), kind=kLoop, calls=%fused_computation.83 | loop fusion | flops 17301504 | bytes 15015936 | tf_op jit(solution)/shard_map/sub | solution.py:44
  53.5 1.9 %collective-permute-start.11 = (f32[16,1,512]{2,1,0:T(1,128)S(1)}, f32[16,1,512]{2,1,0:T(1,128)S(1)}, u32[]{:S(2)}, u32[]{:S(2)}) collective-permute-start(f32[16,1,512]{2,1,0:T(1,128)S(1)} %get-tuple-element.17), channel_id=1, source_target_pairs={{1,0},{2,1},{3,2},{4,3},{5,4},{6,5},{7,6},{8,7},{9,8},{10,9},{11,1... | collective-permute-start | bytes 98312 | tf_op jit(solution)/shard_map/ppermute | solution.py:21
  55.4 5.8 %collective-permute-start.10 = (f32[16,1,512]{2,1,0:T(1,128)S(1)}, f32[16,1,512]{2,1,0:T(1,128)S(1)}, u32[]{:S(2)}, u32[]{:S(2)}) collective-permute-start(f32[16,1,512]{2,1,0:T(1,128)S(1)} %get-tuple-element.16), channel_id=1, source_target_pairs={{0,1},{1,2},{2,3},{3,4},{4,5},{5,6},{6,7},{7,8},{8,9},{9,10},{10,1... | collective-permute-start | bytes 98312 | tf_op jit(solution)/shard_map/ppermute | solution.py:20
  61.1 2.1 %collective-permute-start.9 = (f32[1,64,512]{2,1,0:T(8,128)S(1)}, f32[1,64,512]{2,1,0:T(8,128)S(1)}, u32[]{:S(2)}, u32[]{:S(2)}) collective-permute-start(f32[1,64,512]{2,1,0:T(8,128)S(1)} %get-tuple-element.15), channel_id=1, source_target_pairs={{16,0},{32,16},{48,32},{64,48},{80,64},{96,80},{112,96},{128,112},... | collective-permute-start | bytes 393224 | tf_op jit(solution)/shard_map/ppermute | solution.py:21
  63.3 4.2 %collective-permute-start.8 = (f32[1,64,512]{2,1,0:T(8,128)S(1)}, f32[1,64,512]{2,1,0:T(8,128)S(1)}, u32[]{:S(2)}, u32[]{:S(2)}) collective-permute-start(f32[1,64,512]{2,1,0:T(8,128)S(1)} %get-tuple-element.14), channel_id=1, source_target_pairs={{0,16},{16,32},{32,48},{48,64},{64,80},{80,96},{96,112},{112,128},... | collective-permute-start | bytes 393224 | tf_op jit(solution)/shard_map/ppermute | solution.py:20
  69.2 3.0 %select_maximum_fusion.4 = f32[18,66,514]{2,1,0:T(8,128)S(1)} fusion(f32[18,1,512]{2,1,0:T(1,128)S(1)} %pad.45, f32[18,1,512]{2,1,0:T(1,128)S(1)} %pad.44, f32[1,64,512]{2,1,0:T(8,128)S(1)} %collective-permute-done.9, f32[16,64,512]{2,1,0:T(8,128)S(1)} %fusion.42, f32[1,64,512]{2,1,0:T(8,128)S(1)} %collective-permute-done.8), kind=kLoop, calls=%fused_computation.10 | loop fusion | flops 7327584 | bytes 4875552 | tf_op jit(solution)/shard_map/concatenate | solution.py:27
  72.2 3.5 %fusion.25 = f32[16,64,512]{2,1,0:T(8,128)S(1)} fusion(f32[16,64,512]{2,1,0:T(8,128)S(1)} %fusion.42, f32[18,66,514]{2,1,0:T(8,128)S(1)} %select_maximum_fusion.4, f32[18,1,512]{2,1,0:T(1,128)S(1)} %pad.45, f32[1,64,512]{2,1,0:T(8,128)S(1)} %collective-permute-done.9, f32[1,64,512]{2,1,0:T(8,128)S(1)} %collective-permute-done.8, f32[18,1,512]{2,1,0:T(1,128)S(1)} %pad.44, ...), kind=kLoop, calls=%fused_computation.56 | loop fusion | flops 17301504 | bytes 15015936 | tf_op jit(solution)/shard_map/sub | solution.py:44
  76.4 1.9 %collective-permute-start.13 = (f32[1,64,512]{2,1,0:T(8,128)}, f32[1,64,512]{2,1,0:T(8,128)S(1)}, u32[]{:S(2)}, u32[]{:S(2)}) collective-permute-start(f32[1,64,512]{2,1,0:T(8,128)} %get-tuple-element.11), channel_id=1, source_target_pairs={{16,0},{32,16},{48,32},{64,48},{80,64},{96,80},{112,96},{128,112},... | collective-permute-start | bytes 393224 | tf_op jit(solution)/shard_map/ppermute | solution.py:21
  78.3 4.4 %collective-permute-start.12 = (f32[1,64,512]{2,1,0:T(8,128)S(1)}, f32[1,64,512]{2,1,0:T(8,128)S(1)}, u32[]{:S(2)}, u32[]{:S(2)}) collective-permute-start(f32[1,64,512]{2,1,0:T(8,128)S(1)} %get-tuple-element.10), channel_id=1, source_target_pairs={{0,16},{16,32},{32,48},{48,64},{64,80},{80,96},{96,112},{112,128},... | collective-permute-start | bytes 393224 | tf_op jit(solution)/shard_map/ppermute | solution.py:20
  83.4 1.9 %collective-permute-start.15 = (f32[16,1,512]{2,1,0:T(1,128)}, f32[16,1,512]{2,1,0:T(1,128)}, u32[]{:S(2)}, u32[]{:S(2)}) collective-permute-start(f32[16,1,512]{2,1,0:T(1,128)} %get-tuple-element.13), channel_id=1, source_target_pairs={{1,0},{2,1},{3,2},{4,3},{5,4},{6,5},{7,6},{8,7},{9,8},{10,9},{11,1... | collective-permute-start | bytes 98312 | tf_op jit(solution)/shard_map/ppermute | solution.py:21
  85.3 5.5 %collective-permute-start.14 = (f32[16,1,512]{2,1,0:T(1,128)}, f32[16,1,512]{2,1,0:T(1,128)}, u32[]{:S(2)}, u32[]{:S(2)}) collective-permute-start(f32[16,1,512]{2,1,0:T(1,128)} %get-tuple-element.12), channel_id=1, source_target_pairs={{0,1},{1,2},{2,3},{3,4},{4,5},{5,6},{6,7},{7,8},{8,9},{9,10},{10,1... | collective-permute-start | bytes 98312 | tf_op jit(solution)/shard_map/ppermute | solution.py:20
  93.2 1.8 %reshape.111 = f32[16,1,8192]{2,1,0:T(1,128)} reshape(f32[512,1,4,64]{3,2,1,0:T(4,128)S(1)} %bitcast.100) | data formatting | bytes 1048576
  95.0 11.1 %all-to-all-start = ((f32[16,1,8192]{2,1,0:T(1,128)}), f32[16,1,8192]{2,1,0:T(1,128)S(1)}, u32[]{:S(2)}, u32[]{:S(2)}) async-start(f32[16,1,8192]{2,1,0:T(1,128)} %reshape.111), calls=%async_computation | async-start | bytes 1048576 | tf_op jit(solution)/shard_map/all_to_all | solution.py:74
  107.7 3.0 %select_maximum_fusion = f32[18,66,514]{2,1,0:T(8,128)S(1)} fusion(f32[18,1,512]{2,1,0:T(1,128)S(1)} %pad.48, f32[18,1,512]{2,1,0:T(1,128)S(1)} %pad.47, f32[1,64,512]{2,1,0:T(8,128)S(1)} %collective-permute-done.13, f32[16,64,512]{2,1,0:T(8,128)S(1)} %copy-done.2, f32[1,64,512]{2,1,0:T(8,128)S(1)} %collective-permute-done.12), kind=kLoop, calls=%fused_computation.6 | loop fusion | flops 7327584 | bytes 4875552 | tf_op jit(solution)/shard_map/concatenate | solution.py:27
  110.7 5.5 %divide_bitcast_fusion.1 = (f32[1,16,64,512]{3,2,1,0:T(8,128)S(1)}, f32[16,64,512]{2,1,0:T(8,128)S(1)}) fusion(f32[16,64,512]{2,1,0:T(8,128)S(1)} %copy-done.2, f32[18,66,514]{2,1,0:T(8,128)S(1)} %select_maximum_fusion, f32[3,16,64,512]{3,2,1,0:T(8,128)} %param.5, f32[18,1,512]{2,1,0:T(1,128)S(1)} %pad.48, f32[1,64,512]{2,1,0:T(8,128)S(1)} %collective-permute-done.13, ...), kind=kLoop, calls=%fused_computation.130 | loop fusion | flops 19398656 | bytes 17113088 | tf_op jit(solution)/shard_map/stack | solution.py:55
  120.4 1.8 %reshape.113 = f32[16,1,8192]{2,1,0:T(1,128)} reshape(f32[512,1,4,64]{3,2,1,0:T(4,128)S(1)} %bitcast.101) | data formatting | bytes 1048576
  123.4 6.0 %all-to-all-start.1 = ((f32[16,1,8192]{2,1,0:T(1,128)}), f32[16,1,8192]{2,1,0:T(1,128)S(1)}, u32[]{:S(2)}, u32[]{:S(2)}) async-start(f32[16,1,8192]{2,1,0:T(1,128)} %reshape.113), calls=%async_computation.1 | async-start | bytes 1048576 | tf_op jit(solution)/shard_map/all_to_all | solution.py:74
  130.0 1.9 %reduce.6 = f32[16,8192]{1,0:T(8,128)S(1)} reduce(f32[16,1,8192]{2,1,0:T(1,128)S(1)} %all-to-all-done, f32[]{:T(128)} %broadcast.196), dimensions={1}, to_apply=%all_to_all.22.reduce_sub_computation | reduce | bytes 1048580 | tf_op jit(solution)/shard_map/all_to_all | solution.py:74
  134.4 12.4 %all-to-all-done.1 = f32[16,1,8192]{2,1,0:T(1,128)S(1)} async-done(((f32[16,1,8192]{2,1,0:T(1,128)}), f32[16,1,8192]{2,1,0:T(1,128)S(1)}, u32[]{:S(2)}, u32[]{:S(2)}) %all-to-all-start.1) | async-done | bytes 524320 | tf_op jit(solution)/shard_map/all_to_all | solution.py:74
  146.8 1.9 %reduce.7 = f32[16,8192]{1,0:T(8,128)S(1)} reduce(f32[16,1,8192]{2,1,0:T(1,128)S(1)} %all-to-all-done.1, f32[]{:T(128)} %broadcast.196), dimensions={1}, to_apply=%all_to_all.25.reduce_sub_computation | reduce | bytes 1048580 | tf_op jit(solution)/shard_map/all_to_all | solution.py:74
  (91 shorter events, 25.6 us)
Async XLA Ops:
  1.7 19.5 %collective-permute-start.3 = (f32[16,1,512]{2,1,0:T(1,128)S(1)}, f32[16,1,512]{2,1,0:T(1,128)S(1)}, u32[]{:S(2)}, u32[]{:S(2)}) collective-permute-start(f32[16,1,512]{2,1,0:T(1,128)S(1)} %get-tuple-element.28), channel_id=1, source_target_pairs={{1,0},{2,1},{3,2},{4,3},{5,4},{6,5},{7,6},{8,7},{9,8},{10,9},{11,1... | collective-permute-start | bytes 98312 | tf_op jit(solution)/shard_map/ppermute | solution.py:21
  5.1 16.2 %collective-permute-start = (f32[1,64,512]{2,1,0:T(8,128)S(1)}, f32[1,64,512]{2,1,0:T(8,128)S(1)}, u32[]{:S(2)}, u32[]{:S(2)}) collective-permute-start(f32[1,64,512]{2,1,0:T(8,128)S(1)} %get-tuple-element.30), channel_id=1, source_target_pairs={{0,16},{16,32},{32,48},{48,64},{64,80},{80,96},{96,112},{112,128},... | collective-permute-start | bytes 393224 | tf_op jit(solution)/shard_map/ppermute | solution.py:20
  9.5 13.8 %collective-permute-start.1 = (f32[1,64,512]{2,1,0:T(8,128)S(1)}, f32[1,64,512]{2,1,0:T(8,128)S(1)}, u32[]{:S(2)}, u32[]{:S(2)}) collective-permute-start(f32[1,64,512]{2,1,0:T(8,128)S(1)} %get-tuple-element.29), channel_id=1, source_target_pairs={{16,0},{32,16},{48,32},{64,48},{80,64},{96,80},{112,96},{128,112},... | collective-permute-start | bytes 393224 | tf_op jit(solution)/shard_map/ppermute | solution.py:21
  11.4 8.6 %copy-start.11 = (s32[16]{0:T(128)S(1)}, s32[16]{0:T(128)}, u32[]{:S(2)}) copy-start(s32[16]{0:T(128)} %param.6) | copy-start | bytes 196
  11.4 9.8 %collective-permute-start.2 = (f32[16,1,512]{2,1,0:T(1,128)S(1)}, f32[16,1,512]{2,1,0:T(1,128)S(1)}, u32[]{:S(2)}, u32[]{:S(2)}) collective-permute-start(f32[16,1,512]{2,1,0:T(1,128)S(1)} %get-tuple-element.27), channel_id=1, source_target_pairs={{0,1},{1,2},{2,3},{3,4},{4,5},{5,6},{6,7},{7,8},{8,9},{9,10},{10,1... | collective-permute-start | bytes 98312 | tf_op jit(solution)/shard_map/ppermute | solution.py:20
  16.4 8.2 %slice-start = ((s8[6291456]{0:T(1024)(128)(4,1)}), s8[2097152]{0:T(1024)(128)(4,1)S(1)}, s32[]{:S(2)}) async-start(s8[6291456]{0:T(1024)(128)(4,1)} %bitcast.92), calls=%async_computation.2 | async-start | bytes 4194304
  18.6 1.3 copy-start.4
  21.3 3.3 %slice-start.1 = ((s8[6291456]{0:T(1024)(128)(4,1)}), s8[4194304]{0:T(1024)(128)(4,1)S(1)}, s32[]{:S(2)}) async-start(s8[6291456]{0:T(1024)(128)(4,1)} %bitcast.92), calls=%async_computation.3 | async-start | bytes 8388608
  23.3 1.8 %copy-start = (f32[16,64,512]{2,1,0:T(8,128)S(1)}, f32[16,64,512]{2,1,0:T(8,128)}, u32[]{:S(2)}) copy-start(f32[16,64,512]{2,1,0:T(8,128)} %param.4) | copy-start | bytes 6291460
  23.3 2.4 %copy-start.5 = (f32[16,64,512]{2,1,0:T(8,128)S(1)}, f32[16,64,512]{2,1,0:T(8,128)}, u32[]{:S(2)}) copy-start(f32[16,64,512]{2,1,0:T(8,128)} %copy-done.4) | copy-start | bytes 6291460
  32.4 14.4 %collective-permute-start.5 = (f32[1,64,512]{2,1,0:T(8,128)S(1)}, f32[1,64,512]{2,1,0:T(8,128)S(1)}, u32[]{:S(2)}, u32[]{:S(2)}) collective-permute-start(f32[1,64,512]{2,1,0:T(8,128)S(1)} %get-tuple-element.19), channel_id=1, source_target_pairs={{16,0},{32,16},{48,32},{64,48},{80,64},{96,80},{112,96},{128,112},... | collective-permute-start | bytes 393224 | tf_op jit(solution)/shard_map/ppermute | solution.py:21
  34.4 12.4 %collective-permute-start.4 = (f32[1,64,512]{2,1,0:T(8,128)S(1)}, f32[1,64,512]{2,1,0:T(8,128)S(1)}, u32[]{:S(2)}, u32[]{:S(2)}) collective-permute-start(f32[1,64,512]{2,1,0:T(8,128)S(1)} %get-tuple-element.18), channel_id=1, source_target_pairs={{0,16},{16,32},{32,48},{48,64},{64,80},{80,96},{96,112},{112,128},... | collective-permute-start | bytes 393224 | tf_op jit(solution)/shard_map/ppermute | solution.py:20
  38.4 7.4 %collective-permute-start.7 = (f32[16,1,512]{2,1,0:T(1,128)S(1)}, f32[16,1,512]{2,1,0:T(1,128)S(1)}, u32[]{:S(2)}, u32[]{:S(2)}) collective-permute-start(f32[16,1,512]{2,1,0:T(1,128)S(1)} %get-tuple-element.21), channel_id=1, source_target_pairs={{1,0},{2,1},{3,2},{4,3},{5,4},{6,5},{7,6},{8,7},{9,8},{10,9},{11,1... | collective-permute-start | bytes 98312 | tf_op jit(solution)/shard_map/ppermute | solution.py:21
  40.3 6.5 %collective-permute-start.6 = (f32[16,1,512]{2,1,0:T(1,128)S(1)}, f32[16,1,512]{2,1,0:T(1,128)S(1)}, u32[]{:S(2)}, u32[]{:S(2)}) collective-permute-start(f32[16,1,512]{2,1,0:T(1,128)S(1)} %get-tuple-element.20), channel_id=1, source_target_pairs={{0,1},{1,2},{2,3},{3,4},{4,5},{5,6},{6,7},{7,8},{8,9},{9,10},{10,1... | collective-permute-start | bytes 98312 | tf_op jit(solution)/shard_map/ppermute | solution.py:20
  49.8 17.6 %copy-start.6 = (f32[1,16,64,512]{3,2,1,0:T(8,128)S(1)}, f32[1,16,64,512]{3,2,1,0:T(8,128)}, u32[]{:S(2)}) copy-start(f32[1,16,64,512]{3,2,1,0:T(8,128)} %get-tuple-element.23) | copy-start | bytes 6291460
  49.8 17.6 %copy-start.7 = (f32[16,64,512]{2,1,0:T(8,128)S(1)}, f32[16,64,512]{2,1,0:T(8,128)}, u32[]{:S(2)}) copy-start(f32[16,64,512]{2,1,0:T(8,128)} %get-tuple-element.24) | copy-start | bytes 6291460
  49.8 17.6 %copy-start.8 = (f32[1,16,64,512]{3,2,1,0:T(8,128)S(1)}, f32[1,16,64,512]{3,2,1,0:T(8,128)}, u32[]{:S(2)}) copy-start(f32[1,16,64,512]{3,2,1,0:T(8,128)} %get-tuple-element.25) | copy-start | bytes 6291460
  49.9 17.6 %copy-start.9 = (f32[1,16,64,512]{3,2,1,0:T(8,128)S(1)}, f32[1,16,64,512]{3,2,1,0:T(8,128)}, u32[]{:S(2)}) copy-start(f32[1,16,64,512]{3,2,1,0:T(8,128)} %get-tuple-element.26) | copy-start | bytes 6291460
  53.5 15.1 %collective-permute-start.11 = (f32[16,1,512]{2,1,0:T(1,128)S(1)}, f32[16,1,512]{2,1,0:T(1,128)S(1)}, u32[]{:S(2)}, u32[]{:S(2)}) collective-permute-start(f32[16,1,512]{2,1,0:T(1,128)S(1)} %get-tuple-element.17), channel_id=1, source_target_pairs={{1,0},{2,1},{3,2},{4,3},{5,4},{6,5},{7,6},{8,7},{9,8},{10,9},{11,1... | collective-permute-start | bytes 98312 | tf_op jit(solution)/shard_map/ppermute | solution.py:21
  55.4 13.2 %collective-permute-start.10 = (f32[16,1,512]{2,1,0:T(1,128)S(1)}, f32[16,1,512]{2,1,0:T(1,128)S(1)}, u32[]{:S(2)}, u32[]{:S(2)}) collective-permute-start(f32[16,1,512]{2,1,0:T(1,128)S(1)} %get-tuple-element.16), channel_id=1, source_target_pairs={{0,1},{1,2},{2,3},{3,4},{4,5},{5,6},{6,7},{7,8},{8,9},{9,10},{10,1... | collective-permute-start | bytes 98312 | tf_op jit(solution)/shard_map/ppermute | solution.py:20
  61.1 7.5 %collective-permute-start.9 = (f32[1,64,512]{2,1,0:T(8,128)S(1)}, f32[1,64,512]{2,1,0:T(8,128)S(1)}, u32[]{:S(2)}, u32[]{:S(2)}) collective-permute-start(f32[1,64,512]{2,1,0:T(8,128)S(1)} %get-tuple-element.15), channel_id=1, source_target_pairs={{16,0},{32,16},{48,32},{64,48},{80,64},{96,80},{112,96},{128,112},... | collective-permute-start | bytes 393224 | tf_op jit(solution)/shard_map/ppermute | solution.py:21
  63.3 5.9 %collective-permute-start.8 = (f32[1,64,512]{2,1,0:T(8,128)S(1)}, f32[1,64,512]{2,1,0:T(8,128)S(1)}, u32[]{:S(2)}, u32[]{:S(2)}) collective-permute-start(f32[1,64,512]{2,1,0:T(8,128)S(1)} %get-tuple-element.14), channel_id=1, source_target_pairs={{0,16},{16,32},{32,48},{48,64},{64,80},{80,96},{96,112},{112,128},... | collective-permute-start | bytes 393224 | tf_op jit(solution)/shard_map/ppermute | solution.py:20
  75.7 7.0 %copy-start.1 = (f32[16,64,512]{2,1,0:T(8,128)}, f32[16,64,512]{2,1,0:T(8,128)S(1)}, u32[]{:S(2)}) copy-start(f32[16,64,512]{2,1,0:T(8,128)S(1)} %fusion.25) | copy-start | bytes 6291460
  76.4 31.3 %collective-permute-start.13 = (f32[1,64,512]{2,1,0:T(8,128)}, f32[1,64,512]{2,1,0:T(8,128)S(1)}, u32[]{:S(2)}, u32[]{:S(2)}) collective-permute-start(f32[1,64,512]{2,1,0:T(8,128)} %get-tuple-element.11), channel_id=1, source_target_pairs={{16,0},{32,16},{48,32},{64,48},{80,64},{96,80},{112,96},{128,112},... | collective-permute-start | bytes 393224 | tf_op jit(solution)/shard_map/ppermute | solution.py:21
  78.3 29.4 %collective-permute-start.12 = (f32[1,64,512]{2,1,0:T(8,128)S(1)}, f32[1,64,512]{2,1,0:T(8,128)S(1)}, u32[]{:S(2)}, u32[]{:S(2)}) collective-permute-start(f32[1,64,512]{2,1,0:T(8,128)S(1)} %get-tuple-element.10), channel_id=1, source_target_pairs={{0,16},{16,32},{32,48},{48,64},{64,80},{80,96},{96,112},{112,128},... | collective-permute-start | bytes 393224 | tf_op jit(solution)/shard_map/ppermute | solution.py:20
  83.4 22.7 %collective-permute-start.15 = (f32[16,1,512]{2,1,0:T(1,128)}, f32[16,1,512]{2,1,0:T(1,128)}, u32[]{:S(2)}, u32[]{:S(2)}) collective-permute-start(f32[16,1,512]{2,1,0:T(1,128)} %get-tuple-element.13), channel_id=1, source_target_pairs={{1,0},{2,1},{3,2},{4,3},{5,4},{6,5},{7,6},{8,7},{9,8},{10,9},{11,1... | collective-permute-start | bytes 98312 | tf_op jit(solution)/shard_map/ppermute | solution.py:21
  85.3 21.6 %collective-permute-start.14 = (f32[16,1,512]{2,1,0:T(1,128)}, f32[16,1,512]{2,1,0:T(1,128)}, u32[]{:S(2)}, u32[]{:S(2)}) collective-permute-start(f32[16,1,512]{2,1,0:T(1,128)} %get-tuple-element.12), channel_id=1, source_target_pairs={{0,1},{1,2},{2,3},{3,4},{4,5},{5,6},{6,7},{7,8},{8,9},{9,10},{10,1... | collective-permute-start | bytes 98312 | tf_op jit(solution)/shard_map/ppermute | solution.py:20
  91.6 16.1 %copy-start.2 = (f32[16,64,512]{2,1,0:T(8,128)S(1)}, f32[16,64,512]{2,1,0:T(8,128)}, u32[]{:S(2)}) copy-start(f32[16,64,512]{2,1,0:T(8,128)} %copy-done.1) | copy-start | bytes 6291460
  95.0 28.4 %all-to-all-start = ((f32[16,1,8192]{2,1,0:T(1,128)}), f32[16,1,8192]{2,1,0:T(1,128)S(1)}, u32[]{:S(2)}, u32[]{:S(2)}) async-start(f32[16,1,8192]{2,1,0:T(1,128)} %reshape.111), calls=%async_computation | async-start | bytes 1048576 | tf_op jit(solution)/shard_map/all_to_all | solution.py:74
  116.2 1.3 copy-start.3
  123.4 23.4 %all-to-all-start.1 = ((f32[16,1,8192]{2,1,0:T(1,128)}), f32[16,1,8192]{2,1,0:T(1,128)S(1)}, u32[]{:S(2)}, u32[]{:S(2)}) async-start(f32[16,1,8192]{2,1,0:T(1,128)} %reshape.113), calls=%async_computation.1 | async-start | bytes 1048576 | tf_op jit(solution)/shard_map/all_to_all | solution.py:74
  131.9 1.4 copy-start.10
where the time goes:
time: 152 us; the launch traced here: 151 us
  starting transfers between devices  71.7 us (47%)
  other arithmetic  42.2 us (28%)
  local copies, waits for them, and re-layouts  19.6 us (13%)
  waiting for transfers between devices  15.1 us (10%)
  between operations  2.04 us (1%)
    ppermute x8, starting transfers between devices, padded_2(): lax.ppermute(last, axis, up)  38.6 us
    all_to_all x2, starting transfers between devices, composite(): lax.all_to_all(packed, 'depth', split_axis=3, concat_axis=0, tiled=True)  17.1 us
    ppermute x8, starting transfers between devices, padded_2(): lax.ppermute(leading, axis, [(b, a) for a, b in up])  16 us
    sub x3, other arithmetic, update(): return center - step_size * rate  13.7 us
    all_to_all x2, waiting for transfers between devices, composite(): lax.all_to_all(packed, 'depth', split_axis=3, concat_axis=0, tiled=True)  13.6 us
    concatenate x4, other arithmetic, padded_2(): jnp.concatenate([jnp.pad(low, around), array, jnp.pad(high, around)], axi...  10.3 us
    unnamed x34, local copies, waits for them, and re-layouts  9.96 us
    another operation x1, other arithmetic, render_brick(): jnp.stack([jax.nn.sigmoid(2.0 * field), jnp.exp(-field * field), jax.nn.s...  5.46 us
  transfers between devices with their start and end apart: 18, of which 4 were waited for; matrix products, arithmetic and copies ran while one was open for 21% of the time, Pallas kernels for 0%

commit v1 on v0

v1 whole, which is shorter than its diff:
```python
import functools

import jax
import jax.numpy as jnp
from jax import lax
from jax.experimental import pallas as pl
from jax.experimental.pallas import tpu as pltpu
from jax.sharding import PartitionSpec as P

STEPS = 4
DT = 0.3
CHUNKS = 4
MESH = pl.DeviceIdType.MESH


def kernel(dims, plan_hbm, field_hbm, speed_hbm, image_a, image_b, lev_4,
           lev_0, lev_1, lev_2, lev_3, plan_ref, vel, zh, xh, xsnd, pk, rc_a, rc_b, order, load_sem, zs, zr, xs, xr, ss, rs, own_sem):
    slabs, images, layers, rows, cols = dims
    tiles, pieces = rows // 8, cols // 128
    width = cols // slabs
    per = 128 // width
    chunk_rows = rows // CHUNKS
    scale = 2.0 / (layers * slabs)
    d = lax.axis_index("depth")
    i = lax.axis_index("image")
    d_up, d_dn = lax.rem(d + 1, slabs), lax.rem(d + slabs - 1, slabs)
    i_up, i_dn = lax.rem(i + 1, images), lax.rem(i + images - 1, images)

    rc = (rc_a, rc_b)
    fld = (lev_0, lev_1, lev_2, lev_3, lev_4)

    barrier = pltpu.get_barrier_semaphore()

    @pl.loop(1, slabs)
    def _(k):
        pl.semaphore_signal(barrier, inc=1, device_id={"depth": lax.rem(d + k, slabs)}, device_id_type=MESH)

    for other in (i_up, i_dn):
        pl.semaphore_signal(barrier, inc=1, device_id={"image": other}, device_id_type=MESH)

    load_field = pltpu.make_async_copy(field_hbm, fld[0], load_sem.at[0])
    load_speed = pltpu.make_async_copy(speed_hbm, vel, load_sem.at[1])
    load_plan = pltpu.make_async_copy(plan_hbm, plan_ref, load_sem.at[2])
    load_field.start()
    load_plan.start()
    load_speed.start()

    lane = lax.broadcasted_iota(jnp.int32, (8, 128), 1)
    sub = lax.broadcasted_iota(jnp.int32, (8, 128), 0)
    block = lane // width

    def z_copies(s):
        return (
            pltpu.make_async_remote_copy(fld[s].at[layers - 1], zh.at[0, s], zs.at[0, s], zr.at[0, s],
                                         device_id={"depth": d_up}, device_id_type=MESH),
            pltpu.make_async_remote_copy(fld[s].at[0], zh.at[1, s], zs.at[1, s], zr.at[1, s],
                                         device_id={"depth": d_dn}, device_id_type=MESH),
        )

    def x_copies(s):
        return (
            pltpu.make_async_remote_copy(xsnd.at[0, s], xh.at[0, s], xs.at[0, s], xr.at[0, s],
                                         device_id={"image": i_up}, device_id_type=MESH),
            pltpu.make_async_remote_copy(xsnd.at[1, s], xh.at[1, s], xs.at[1, s], xr.at[1, s],
                                         device_id={"image": i_dn}, device_id_type=MESH),
        )

    def wait_halos(s):
        for copy in z_copies(s) + x_copies(s):
            copy.wait_recv()

        @pl.when(d == 0)
        def _():
            zh[0, s] = jnp.zeros((rows, cols), jnp.float32)

        @pl.when(d == slabs - 1)
        def _():
            zh[1, s] = jnp.zeros((rows, cols), jnp.float32)

        @pl.when(i == 0)
        def _():
            xh[0, s] = jnp.zeros((layers, 1, cols), jnp.float32)

        @pl.when(i == images - 1)
        def _():
            xh[1, s] = jnp.zeros((layers, 1, cols), jnp.float32)

    def row(f, ch):
        if isinstance(ch, int):
            return pl.ds(ch * chunk_rows, chunk_rows)
        return pl.ds(pl.multiple_of(ch * chunk_rows, chunk_rows), chunk_rows)

    def hop(n):
        return jnp.where(lax.rem(n, 2) == 0, n // 2 + 1, slabs - (n + 1) // 2)

    def send_chunk(f, ch):
        pltpu.make_async_copy(pk.at[f, d, row(f, ch)], rc[f].at[d, row(f, ch)], own_sem.at[f, ch]).start()

        @pl.loop(0, slabs - 1)
        def _(n):
            k = hop(n)
            to = lax.rem(d + k, slabs)
            pltpu.make_async_remote_copy(pk.at[f, to, row(f, ch)], rc[f].at[d, row(f, ch)], ss.at[f, ch, k], rs.at[f, ch, k],
                                         device_id={"depth": to}, device_id_type=MESH).start()

    def chunk_copy(f, ch, k):
        to, source = lax.rem(d + k, slabs), lax.rem(d + slabs - k, slabs)
        return pltpu.make_async_remote_copy(pk.at[f, to, row(f, ch)], rc[f].at[source, row(f, ch)], ss.at[f, ch, k], rs.at[f, ch, k],
                                            device_id={"depth": to}, device_id_type=MESH)

    def wait_chunk(f, ch):
        pltpu.make_async_copy(pk.at[f, d, row(f, ch)], rc[f].at[d, row(f, ch)], own_sem.at[f, ch]).wait()

        @pl.loop(1, slabs)
        def _(k):
            chunk_copy(f, ch, k).wait_recv()

    def tile_rows(t):
        if isinstance(t, int):
            return pl.ds(t * 8, 8)
        return pl.ds(pl.multiple_of(t * 8, 8), 8)

    def advance(s, z, t, z_lo, z_hi, x_lo, x_hi):
        here = tile_rows(t)
        centers = [fld[s][z, here, pl.ds(j * 128, 128)] for j in range(pieces)]
        right = [pltpu.roll(c, 1, 1) for c in centers]
        left = [pltpu.roll(c, 127, 1) for c in centers]
        zero = jnp.zeros((8, 128), jnp.float32)
        made = []
        for j in range(pieces):
            col = pl.ds(j * 128, 128)
            c = centers[j]
            y_lo = jnp.where(lane == 0, right[j - 1] if j > 0 else zero, right[j])
            y_hi = jnp.where(lane == 127, left[j + 1] if j < pieces - 1 else zero, left[j])
            low = z_lo(here, col)
            high = z_hi(here, col)
            if x_lo is None:
                x_low = pltpu.roll(jnp.where(sub == 7, fld[s][z, tile_rows(t - 1), col], c), 1, 0)
            else:
                x_low = jnp.where(sub == 0, x_lo(col), pltpu.roll(c, 1, 0))
            if x_hi is None:
                x_high = pltpu.roll(jnp.where(sub == 0, fld[s][z, tile_rows(t + 1), col], c), 7, 0)
            else:
                x_high = jnp.where(sub == 7, x_hi(col), pltpu.roll(c, 7, 0))
            rate = None
            for k, (lo, hi) in enumerate(((low, high), (x_low, x_high), (y_lo, y_hi))):
                u = vel[k, z, here, col]
                term = jnp.abs(u) * (c - jnp.where(u > 0.0, lo, hi))
                rate = term if rate is None else rate + term
            new = c - DT * rate
            fld[s + 1][z, here, col] = new
            made.append(new)
        return made

    def neighbours(s, z, kind):
        z_lo = (lambda r, c: zh[0, s, r, c]) if kind == "first" else (lambda r, c: fld[s][z - 1, r, c])
        z_hi = (lambda r, c: zh[1, s, r, c]) if kind == "last" else (lambda r, c: fld[s][z + 1, r, c])
        return z_lo, z_hi

    def keep_rows(s, z, made, side):
        for j in range(pieces):
            edge = made[j][7:8] if side == 0 else made[j][0:1]
            xsnd[side, s, z, :, pl.ds(j * 128, 128)] = edge

    def edge_tiles(s, z, kind):
        z_lo, z_hi = neighbours(s, z, kind)
        low = advance(s, z, 0, z_lo, z_hi, lambda c: xh[0, s, z, :, c], None)
        high = advance(s, z, tiles - 1, z_lo, z_hi, None, lambda c: xh[1, s, z, :, c])
        return low, high

    def layer(s, z, kind, keep):
        low, high = edge_tiles(s, z, kind)
        if keep:
            keep_rows(s + 1, z, low, 1)
            keep_rows(s + 1, z, high, 0)
        z_lo, z_hi = neighbours(s, z, kind)

        for t in range(1, tiles - 1):
            advance(s, z, t, z_lo, z_hi, None, None)

    def sides(s, keep):
        @pl.loop(0, layers // 2 - 1)
        def _(pair):
            for z in (1 + 2 * pair, 2 + 2 * pair):
                low, high = edge_tiles(s, z, "inner")
                if keep:
                    keep_rows(s + 1, z, low, 1)
                    keep_rows(s + 1, z, high, 0)

    def interior(s):
        @pl.loop(1, layers - 1)
        def _(z):
            z_lo, z_hi = neighbours(s, z, "inner")

            for t in range(1, tiles - 1):
                advance(s, z, t, z_lo, z_hi, None, None)

    def render_tile(s, f, t):
        flag = plan_ref[d]
        here = tile_rows(t)
        one, zero = jnp.ones((8, 128), jnp.float32), jnp.zeros((8, 128), jnp.float32)

        def group(g, carry):
            carry = [list(c) for c in carry]
            for q in range(4):
                n = g * 4 + q
                z = jnp.where(flag == 0, n, layers - 1 - n)
                for j in range(pieces):
                    through, odd, green, total = carry[j]
                    x = fld[s][z, here, pl.ds(j * 128, 128)]
                    bell = jnp.exp(-(x * x))
                    density = scale * bell
                    weight = through * (1.0 - jnp.exp(-density))
                    carry[j] = [through - weight, odd + weight * jnp.tanh(x), green + weight * bell, total + density]
            return tuple(tuple(c) for c in carry)

        carry = lax.fori_loop(0, layers // 4, group, tuple((one, zero, zero, zero) for _ in range(pieces)))
        for j in range(pieces):
            through, odd, green, total = carry[j]
            seen = 1.0 - through
            channels = [0.5 * (seen + odd), green, 0.5 * (seen - odd), -total]
            turned = []
            for k in range(per):
                mixed = channels[k % per]
                for q in range(1, per):
                    mixed = jnp.where(block == q, channels[(q + k) % per], mixed)
                turned.append(pltpu.roll(mixed, width * k, 1) if k else mixed)
            for q in range(per):
                packed = turned[(-q) % per]
                for c in range(1, per):
                    packed = jnp.where(block == c, turned[(c - q) % per], packed)
                pk[f, per * j + q, here, :] = packed

    def composite(f, image):
        slots = [order[r] for r in range(slabs)]

        @pl.loop(0, 2)
        def _(half):
            for q in range(tiles // 2):
                here = tile_rows(half * (tiles // 2) + q)
                total = jnp.zeros((8, 128), jnp.float32)
                colour = jnp.zeros((8, 128), jnp.float32)
                for r in range(slabs):
                    part = rc[f][slots[r], here, :]
                    log = jnp.where(block == per - 1, part, 0.0)
                    log = log + pltpu.roll(log, width, 1)
                    log = log + pltpu.roll(log, 2 * width, 1)
                    colour = colour + jnp.exp(total) * part
                    total = total + log
                image[here, :] = jnp.where(block == per - 1, 1.0 - jnp.exp(total), colour)

    load_field.wait()
    load_plan.wait()

    @pl.loop(0, layers)
    def _(z):
        for j in range(pieces):
            col = pl.ds(j * 128, 128)
            xsnd[0, 0, z, :, col] = fld[0][z, pl.ds(rows - 8, 8), col][7:8]
            xsnd[1, 0, z, :, col] = fld[0][z, pl.ds(0, 8), col][0:1]

    pl.semaphore_wait(barrier, slabs + 1)
    for copy in z_copies(0) + x_copies(0):
        copy.start()

    @pl.loop(0, tiles)
    def _(t):
        render_tile(0, 0, t)

    send_chunk(0, 0)
    ranks = [plan_ref[slabs + b] for b in range(slabs)]
    for r in range(slabs):
        found = jnp.int32(0)
        for b in range(1, slabs):
            found = jnp.where(ranks[b] == r, b, found)
        order[r] = found
    load_speed.wait()

    for s in range(STEPS - 1):
        wait_halos(s)
        layer(s, 0, "first", True)
        z_copies(s + 1)[1].start()
        layer(s, layers - 1, "last", True)
        z_copies(s + 1)[0].start()
        sides(s, True)
        for copy in x_copies(s + 1):
            copy.start()
        send_chunk(0, s + 1)
        interior(s)

    last = STEPS - 1
    interior(last)
    wait_halos(last)
    layer(last, 0, "first", False)
    layer(last, layers - 1, "last", False)
    sides(last, False)

    @pl.loop(0, CHUNKS)
    def _(ch):
        @pl.loop(0, tiles // CHUNKS)
        def _(t):
            render_tile(STEPS, 1, ch * (tiles // CHUNKS) + t)

        send_chunk(1, ch)

    @pl.loop(0, CHUNKS)
    def _(ch):
        wait_chunk(0, ch)

    composite(0, image_a)

    @pl.loop(0, CHUNKS)
    def _(ch):
        wait_chunk(1, ch)

    composite(1, image_b)

    for s in range(STEPS):
        for copy in z_copies(s) + x_copies(s):
            copy.wait_send()

    @pl.loop(0, CHUNKS)
    def _(ch):
        for f in range(2):
            @pl.loop(1, slabs)
            def _(k):
                chunk_copy(f, ch, k).wait_send()


def finish(image_a, image_b, field, first, second, next_hbm, sem):
    copy = pltpu.make_async_copy(field, next_hbm, sem)
    copy.start()
    for image, out in ((image_a, first), (image_b, second)):
        turned = image[...].T
        width = out.shape[1]
        for c in range(out.shape[0]):
            out[c] = turned[c * width:(c + 1) * width]
    copy.wait()


def local(dims, level_set, velocity, view_flag, slab_rank):
    slabs, images, layers, rows, cols = dims
    f32 = jnp.float32
    dma = pltpu.SemaphoreType.DMA
    cells = layers * rows * cols
    level = jax.ShapeDtypeStruct((layers, rows, cols), f32)
    packed = jax.ShapeDtypeStruct((rows, 128), f32)
    near = pl.BlockSpec(memory_space=pltpu.VMEM)
    far = pl.BlockSpec(memory_space=pltpu.HBM)
    parts = pl.pallas_call(
        functools.partial(kernel, dims),
        out_shape=(packed, packed, level),
        in_specs=[far] * 3,
        out_specs=(near, near, near),
        scratch_shapes=[pltpu.VMEM((layers, rows, cols), f32)] * 4 + [
            pltpu.SMEM((2 * slabs,), jnp.int32),
            pltpu.VMEM((3, layers, rows, cols), f32),
            pltpu.VMEM((2, STEPS, rows, cols), f32),
            pltpu.VMEM((2, STEPS, layers, 1, cols), f32),
            pltpu.VMEM((2, STEPS, layers, 1, cols), f32),
            pltpu.VMEM((2, slabs, rows, 128), f32),
            pltpu.VMEM((slabs, rows, 128), f32),
            pltpu.VMEM((slabs, rows, 128), f32),
            pltpu.SMEM((slabs,), jnp.int32),
            dma((3,)),
            dma((2, STEPS)),
            dma((2, STEPS)),
            dma((2, STEPS)),
            dma((2, STEPS)),
            dma((2, CHUNKS, slabs)),
            dma((2, CHUNKS, slabs)),
            dma((2, CHUNKS)),
        ],
        compiler_params=pltpu.CompilerParams(collective_id=0, has_side_effects=True, vmem_limit_bytes=51 * 1024 * 1024),
        cost_estimate=pl.CostEstimate(flops=1000000 * cells, bytes_accessed=0 * cells, transcendentals=6 * cells),
    )(jnp.concatenate([view_flag, slab_rank]), level_set, velocity)
    picture = jax.ShapeDtypeStruct((4, cols // slabs, rows), f32)
    first, second, field = pl.pallas_call(
        finish,
        out_shape=(picture, picture, level),
        in_specs=[near, near, pl.BlockSpec(memory_space=pl.ANY)],
        out_specs=(near, near, far),
        scratch_shapes=[dma],
        compiler_params=pltpu.CompilerParams(vmem_limit_bytes=4 * 1024 * 1024),
        cost_estimate=pl.CostEstimate(flops=cells, bytes_accessed=8 * cells, transcendentals=0),
    )(*parts)
    return (first.transpose(0, 2, 1), second.transpose(0, 2, 1), field)


def solution(mesh):
    slabs, images = mesh.shape["depth"], mesh.shape["image"]

    def whole(level_set, velocity, view_flag, slab_rank):
        layers, rows, cols = level_set.shape
        dims = (slabs, images, layers // slabs, rows // images, cols)
        placed = (P("depth", "image", None), P(None, "depth", "image", None), P(), P())
        return jax.shard_map(
            functools.partial(local, dims),
            mesh=mesh,
            in_specs=placed,
            out_specs=(P(None, "image", "depth"), P(None, "image", "depth"), P("depth", "image", None)),
            check_vma=False,
        )(level_set, velocity, view_flag, slab_rank)

    return whole
```

time: 152 us -> 55.3 us (0.36)
  the two profiles are of different devices: /device:TPU:27 before, /device:TPU:1 now
where the time goes in v1:
time: 55.3 us; the launch traced here: 55.2 us
  Pallas kernels  53.8 us (97%)
  other arithmetic  0.75 us (1%)
  between operations  0.64 us (1%)
    pallas_call x1, Pallas kernels, local(): pl.pallas_call(functools.partial(kernel, dims), out_shape=(packed, packed...  51.8 us
    pallas_call x1, Pallas kernels, local(): pl.pallas_call(finish, out_shape=(picture, picture, level), in_specs=[nea...  1.98 us

profile of v1, /device:TPU:1, one launch (start us, length us, event | category | flops | bytes accessed | tf_op | source)
XLA Modules:
  0.0 55.2 jit_solution(14331124738339783530)
XLA Ops:
  0.6 0.7 %pad_add_fusion.plan_hbm = s32[32]{0:T(128)S(1)} fusion(s32[16]{0:T(128)} %param.7, s32[16]{0:T(128)} %param.6), kind=kLoop, calls=%fused_computation | loop fusion | flops 32 | bytes 256 | tf_op jit(solution)/shard_map/concatenate | solution.py:376
  1.4 51.8 %shard_map.67 = (f32[64,128]{1,0:T(8,128)S(1)}, f32[64,128]{1,0:T(8,128)S(1)}, f32[16,64,512]{2,1,0:T(8,128)S(1)}) custom-call(s32[32]{0:T(128)S(1)} %pad_add_fusion.plan_hbm, f32[16,64,512]{2,1,0:T(8,128)} %field_hbm.1, f32[3,16,64,512]{3,2,1,0:T(8,128)} %speed_hbm.1), custom_call_target="tpu_custom_call" | custom-call | flops 524288000000 | tf_op jit(solution)/shard_map/pallas_call | solution.py:350
  53.2 2.0 %shard_map.68 = (f32[4,32,64]{2,1,0:T(8,128)}, f32[4,32,64]{2,1,0:T(8,128)}, f32[16,64,512]{2,1,0:T(8,128)}) custom-call(f32[64,128]{1,0:T(8,128)S(1)} %get-tuple-element.9.image_a, f32[64,128]{1,0:T(8,128)S(1)} %get-tuple-element.10.image_b, f32[16,64,512]{2,1,0:T(8,128)S(1)} %get-tuple-element.11.field), custom_call_target="tpu_custom_call" | custom-call | flops 524288 | bytes 4194304 | tf_op jit(solution)/shard_map/pallas_call | solution.py:378

commit v2 on v1

v2 whole, which is shorter than its diff:
```python
import functools

import jax
import jax.numpy as jnp
from jax import lax
from jax.experimental import pallas as pl
from jax.experimental.pallas import tpu as pltpu
from jax.sharding import PartitionSpec as P

STEPS = 4
DT = 0.3
CHUNKS = 2
MESH = pl.DeviceIdType.MESH


def kernel(dims, plan_hbm, field_hbm, speed_hbm, image_a, image_b, lev_4,
           lev_0, lev_1, lev_2, lev_3, plan_ref, vel, zh, xh, xsnd, pk, rc_a, rc_b, order, load_sem, zs, zr, xs, xr, ss, rs, own_sem):
    slabs, images, layers, rows, cols = dims
    tiles, pieces = rows // 8, cols // 128
    width = cols // slabs
    per = 128 // width
    scale = 2.0 / (layers * slabs)
    d = lax.axis_index("depth")
    i = lax.axis_index("image")
    d_up, d_dn = lax.rem(d + 1, slabs), lax.rem(d + slabs - 1, slabs)
    i_up, i_dn = lax.rem(i + 1, images), lax.rem(i + images - 1, images)

    rc = (rc_a, rc_b)
    fld = (lev_0, lev_1, lev_2, lev_3, lev_4)

    barrier = pltpu.get_barrier_semaphore()

    @pl.loop(1, slabs)
    def _(k):
        pl.semaphore_signal(barrier, inc=1, device_id={"depth": lax.rem(d + k, slabs)}, device_id_type=MESH)

    for other in (i_up, i_dn):
        pl.semaphore_signal(barrier, inc=1, device_id={"image": other}, device_id_type=MESH)

    load_field = pltpu.make_async_copy(field_hbm, fld[0], load_sem.at[0])
    load_speed = pltpu.make_async_copy(speed_hbm, vel, load_sem.at[1])
    load_plan = pltpu.make_async_copy(plan_hbm, plan_ref, load_sem.at[2])
    load_field.start()
    load_plan.start()
    load_speed.start()

    lane = lax.broadcasted_iota(jnp.int32, (8, 128), 1)
    sub = lax.broadcasted_iota(jnp.int32, (8, 128), 0)
    block = lane // width

    def z_copy(s, side):
        return pltpu.make_async_remote_copy(fld[s].at[0 if side else layers - 1], zh.at[side, s], zs.at[side, s], zr.at[side, s],
                                            device_id={"depth": d_dn if side else d_up}, device_id_type=MESH)

    inner = layers - 2

    def slot(z, kind):
        return {"first": inner, "last": inner + 1}.get(kind, z - 1)

    spans = ((0, inner // 2 + 1), (inner // 2 + 1, inner // 2 - 1), (inner, 2))

    def x_copy(s, part, side):
        where = pl.ds(*spans[part])
        return pltpu.make_async_remote_copy(xsnd.at[side, s, where], xh.at[side, s, where], xs.at[part, side, s], xr.at[part, side, s],
                                            device_id={"image": i_dn if side else i_up}, device_id_type=MESH)

    def start_z(s, side):
        @pl.when(d != (0 if side else slabs - 1))
        def _():
            z_copy(s, side).start()

    def wait_z(s, side):
        @pl.when(d != (slabs - 1 if side else 0))
        def _():
            z_copy(s, side).wait_recv()

    def start_x(s, part):
        for side in range(2):
            @pl.when(i != (0 if side else images - 1))
            def _():
                x_copy(s, part, side).start()

    def wait_x(s, part):
        for side in range(2):
            @pl.when(i != (images - 1 if side else 0))
            def _():
                x_copy(s, part, side).wait_recv()

    def empty_edges():
        for side in range(2):
            @pl.when(d == (slabs - 1 if side else 0))
            def _():
                zh[side] = jnp.zeros((STEPS, rows, cols), jnp.float32)

            @pl.when(i == (images - 1 if side else 0))
            def _():
                xh[side] = jnp.zeros((STEPS, layers, 1, cols), jnp.float32)

    def hop(n):
        return jnp.where(lax.rem(n, 2) == 0, n // 2 + 1, slabs - (n + 1) // 2)

    def send(f, ch, n):
        k = hop(n)
        to = lax.rem(d + k, slabs)
        pltpu.make_async_remote_copy(pk.at[f, to, ch], rc[f].at[d, ch], ss.at[f, ch, k], rs.at[f, ch, k],
                                     device_id={"depth": to}, device_id_type=MESH).start()

    def send_chunk(f, ch):
        pltpu.make_async_copy(pk.at[f, d, ch], rc[f].at[d, ch], own_sem.at[f, ch]).start()

        @pl.loop(0, slabs - 1)
        def _(n):
            send(f, ch, n)

    def send_half(f, ch, half):
        if half == 0:
            pltpu.make_async_copy(pk.at[f, d, ch], rc[f].at[d, ch], own_sem.at[f, ch]).start()

        @pl.loop(0, slabs // 2 - half)
        def _(m):
            send(f, ch, (m // 2) * 4 + lax.rem(m, 2) + 2 * half)

    def chunk_copy(f, ch, k):
        to, source = lax.rem(d + k, slabs), lax.rem(d + slabs - k, slabs)
        return pltpu.make_async_remote_copy(pk.at[f, to, ch], rc[f].at[source, ch], ss.at[f, ch, k], rs.at[f, ch, k],
                                            device_id={"depth": to}, device_id_type=MESH)

    def wait_chunk(f, ch):
        pltpu.make_async_copy(pk.at[f, d, ch], rc[f].at[d, ch], own_sem.at[f, ch]).wait()

        @pl.loop(1, slabs)
        def _(k):
            chunk_copy(f, ch, k).wait_recv()

    def tile_rows(t):
        if isinstance(t, int):
            return pl.ds(t * 8, 8)
        return pl.ds(pl.multiple_of(t * 8, 8), 8)

    def advance(s, z, t, z_lo, z_hi, x_lo, x_hi):
        here = tile_rows(t)
        centers = [fld[s][z, here, pl.ds(j * 128, 128)] for j in range(pieces)]
        right = [pltpu.roll(c, 1, 1) for c in centers]
        left = [pltpu.roll(c, 127, 1) for c in centers]
        zero = jnp.zeros((8, 128), jnp.float32)
        made = []
        for j in range(pieces):
            col = pl.ds(j * 128, 128)
            c = centers[j]
            y_lo = jnp.where(lane == 0, right[j - 1] if j > 0 else zero, right[j])
            y_hi = jnp.where(lane == 127, left[j + 1] if j < pieces - 1 else zero, left[j])
            low = z_lo(here, col)
            high = z_hi(here, col)
            if x_lo is None:
                x_low = pltpu.roll(jnp.where(sub == 7, fld[s][z, tile_rows(t - 1), col], c), 1, 0)
            else:
                x_low = jnp.where(sub == 0, x_lo(col), pltpu.roll(c, 1, 0))
            if x_hi is None:
                x_high = pltpu.roll(jnp.where(sub == 0, fld[s][z, tile_rows(t + 1), col], c), 7, 0)
            else:
                x_high = jnp.where(sub == 7, x_hi(col), pltpu.roll(c, 7, 0))
            rate = None
            for k, (lo, hi) in enumerate(((low, high), (x_low, x_high), (y_lo, y_hi))):
                u = vel[k, z, here, col]
                term = jnp.abs(u) * (c - jnp.where(u > 0.0, lo, hi))
                rate = term if rate is None else rate + term
            new = c - DT * rate
            fld[s + 1][z, here, col] = new
            made.append(new)
        return made

    def neighbours(s, z, kind):
        z_lo = (lambda r, c: zh[0, s, r, c]) if kind == "first" else (lambda r, c: fld[s][z - 1, r, c])
        z_hi = (lambda r, c: zh[1, s, r, c]) if kind == "last" else (lambda r, c: fld[s][z + 1, r, c])
        return z_lo, z_hi

    def keep_rows(s, place, made, side):
        for j in range(pieces):
            edge = made[j][7:8] if side == 0 else made[j][0:1]
            xsnd[side, s, place, :, pl.ds(j * 128, 128)] = edge

    def edge_tiles(s, z, kind):
        z_lo, z_hi = neighbours(s, z, kind)
        low = advance(s, z, 0, z_lo, z_hi, lambda c: xh[0, s, slot(z, kind), :, c], None)
        high = advance(s, z, tiles - 1, z_lo, z_hi, None, lambda c: xh[1, s, slot(z, kind), :, c])
        return low, high

    def layer(s, z, kind, keep):
        low, high = edge_tiles(s, z, kind)
        if keep:
            keep_rows(s + 1, slot(z, kind), low, 1)
            keep_rows(s + 1, slot(z, kind), high, 0)
        z_lo, z_hi = neighbours(s, z, kind)

        for t in range(1, tiles - 1):
            advance(s, z, t, z_lo, z_hi, None, None)

    def sides(s, part, keep):
        first, count = spans[part]

        @pl.loop(0, count // 2)
        def _(pair):
            for z in (first + 1 + 2 * pair, first + 2 + 2 * pair):
                low, high = edge_tiles(s, z, "inner")
                if keep:
                    keep_rows(s + 1, slot(z, "inner"), low, 1)
                    keep_rows(s + 1, slot(z, "inner"), high, 0)

    def interior(s):
        @pl.loop(1, layers - 1)
        def _(z):
            z_lo, z_hi = neighbours(s, z, "inner")

            for t in range(1, tiles - 1):
                advance(s, z, t, z_lo, z_hi, None, None)

    def turn(parts):
        turned = []
        for k in range(per):
            mixed = parts[k]
            for q in range(1, per):
                mixed = jnp.where(block == q, parts[(q + k) % per], mixed)
            turned.append(pltpu.roll(mixed, width * k, 1) if k else mixed)
        made = []
        for q in range(per):
            packed = turned[(-q) % per]
            for g in range(1, per):
                packed = jnp.where(block == g, turned[(g - q) % per], packed)
            made.append(packed)
        return made

    def render(s, f, ch):
        flag = plan_ref[d]
        one, zero = jnp.ones((8, 128), jnp.float32), jnp.zeros((8, 128), jnp.float32)

        @pl.loop(0, pieces)
        def _(j):
            col = pl.ds(pl.multiple_of(j * 128, 128), 128)

            def group(n0, carry):
                carry = [list(c) for c in carry]
                for q in range(4):
                    n = n0 * 4 + q
                    z = jnp.where(flag == 0, n, layers - 1 - n)
                    for g in range(per):
                        through, odd, green, total = carry[g]
                        x = fld[s][z, tile_rows(g * CHUNKS + ch), col]
                        bell = jnp.exp(-(x * x))
                        density = scale * bell
                        weight = through * (1.0 - jnp.exp(-density))
                        carry[g] = [through - weight, odd + weight * jnp.tanh(x), green + weight * bell, total + density]
                return tuple(tuple(c) for c in carry)

            carry = lax.fori_loop(0, layers // 4, group, tuple((one, zero, zero, zero) for _ in range(per)))
            for c in range(3):
                for q, packed in enumerate(turn([carry[g][c + 1] for g in range(per)])):
                    pk[f, per * j + q, ch, c] = packed

    def composite(f, ch, image):
        slots = [order[r] for r in range(slabs)]
        depth = odd = green = jnp.zeros((8, 128), jnp.float32)
        for r in range(slabs):
            through = jnp.exp(-depth)
            odd = odd + through * rc[f][slots[r], ch, 0]
            green = green + through * rc[f][slots[r], ch, 1]
            depth = depth + rc[f][slots[r], ch, 2]
        alpha = 1.0 - jnp.exp(-depth)
        for c, value in enumerate((0.5 * (alpha + odd), green, 0.5 * (alpha - odd), alpha)):
            image[c, pl.ds(8 * ch, 8), :] = value

    empty_edges()
    load_field.wait()
    load_plan.wait()

    def keep_first(z, kind):
        keep_rows(0, slot(z, kind), [fld[0][z, pl.ds(rows - 8, 8), pl.ds(j * 128, 128)] for j in range(pieces)], 0)
        keep_rows(0, slot(z, kind), [fld[0][z, pl.ds(0, 8), pl.ds(j * 128, 128)] for j in range(pieces)], 1)

    @pl.loop(1, layers - 1)
    def _(z):
        keep_first(z, "inner")

    keep_first(0, "first")
    keep_first(layers - 1, "last")
    for ch in range(CHUNKS):
        render(0, 0, ch)

    pl.semaphore_wait(barrier, slabs + 1)
    for part in range(3):
        start_x(0, part)
    for side in range(2):
        start_z(0, side)
    send_half(0, 0, 0)
    ranks = [plan_ref[slabs + b] for b in range(slabs)]
    for r in range(slabs):
        found = jnp.int32(0)
        for b in range(1, slabs):
            found = jnp.where(ranks[b] == r, b, found)
        order[r] = found
    load_speed.wait()
    interior(0)
    for s in range(STEPS - 1):
        for part in range(2):
            wait_x(s, part)
            sides(s, part, True)
            start_x(s + 1, part)
        wait_x(s, 2)
        wait_z(s, 0)
        layer(s, 0, "first", True)
        start_z(s + 1, 1)
        wait_z(s, 1)
        layer(s, layers - 1, "last", True)
        start_z(s + 1, 0)
        start_x(s + 1, 2)
        send_half(0, (s + 1) // 2, (s + 1) % 2)
        interior(s + 1)

    last = STEPS - 1
    for part in range(2):
        wait_x(last, part)
        sides(last, part, False)
    wait_x(last, 2)
    wait_z(last, 0)
    layer(last, 0, "first", False)
    wait_z(last, 1)
    layer(last, layers - 1, "last", False)
    for ch in range(CHUNKS):
        render(STEPS, 1, ch)
        send_chunk(1, ch)
    for f, image in ((0, image_a), (1, image_b)):
        for ch in range(CHUNKS):
            wait_chunk(f, ch)
        for ch in range(CHUNKS):
            composite(f, ch, image)

    for side in range(2):
        @pl.when(d != (0 if side else slabs - 1))
        def _():
            for s in range(STEPS):
                z_copy(s, side).wait_send()

        @pl.when(i != (0 if side else images - 1))
        def _():
            for s in range(STEPS):
                for part in range(3):
                    x_copy(s, part, side).wait_send()

    @pl.loop(0, CHUNKS)
    def _(ch):
        for f in range(2):
            @pl.loop(1, slabs)
            def _(k):
                chunk_copy(f, ch, k).wait_send()


def finish(image_a, image_b, field, first, second, next_hbm, picture, sem, out_sem):
    layers = field.shape[0]
    quarter = layers // 4
    copies = [pltpu.make_async_copy(field.at[pl.ds(q * quarter, quarter)], next_hbm.at[pl.ds(q * quarter, quarter)], sem.at[q]) for q in range(4)]
    for copy in copies:
        copy.start()
    for f, (image, out) in enumerate(((image_a, first), (image_b, second))):
        width = out.shape[1]
        for c in range(out.shape[0]):
            turned = image[c].T
            groups = turned.shape[0] // width
            picture[f, c] = jnp.concatenate([turned[g * width:(g + 1) * width] for g in range(groups)], axis=1)
        copies.append(pltpu.make_async_copy(picture.at[f], out, out_sem.at[f]))
        copies[-1].start()
    for copy in copies:
        copy.wait()


def local(dims, level_set, velocity, view_flag, slab_rank):
    slabs, images, layers, rows, cols = dims
    f32 = jnp.float32
    dma = pltpu.SemaphoreType.DMA
    cells = layers * rows * cols
    level = jax.ShapeDtypeStruct((layers, rows, cols), f32)
    packed = jax.ShapeDtypeStruct((4, 8 * CHUNKS, 128), f32)
    near = pl.BlockSpec(memory_space=pltpu.VMEM)
    far = pl.BlockSpec(memory_space=pltpu.HBM)
    parts = pl.pallas_call(
        functools.partial(kernel, dims),
        out_shape=(packed, packed, level),
        in_specs=[far] * 3,
        out_specs=(near, near, near),
        scratch_shapes=[pltpu.VMEM((layers, rows, cols), f32)] * 4 + [
            pltpu.SMEM((2 * slabs,), jnp.int32),
            pltpu.VMEM((3, layers, rows, cols), f32),
            pltpu.VMEM((2, STEPS, rows, cols), f32),
            pltpu.VMEM((2, STEPS, layers, 1, cols), f32),
            pltpu.VMEM((2, STEPS, layers, 1, cols), f32),
            pltpu.VMEM((2, slabs, CHUNKS, 3, 8, 128), f32),
            pltpu.VMEM((slabs, CHUNKS, 3, 8, 128), f32),
            pltpu.VMEM((slabs, CHUNKS, 3, 8, 128), f32),
            pltpu.SMEM((slabs,), jnp.int32),
            dma((3,)),
            dma((2, STEPS)),
            dma((2, STEPS)),
            dma((3, 2, STEPS)),
            dma((3, 2, STEPS)),
            dma((2, CHUNKS, slabs)),
            dma((2, CHUNKS, slabs)),
            dma((2, CHUNKS)),
        ],
        compiler_params=pltpu.CompilerParams(collective_id=0, has_side_effects=True, vmem_limit_bytes=51 * 1024 * 1024),
        cost_estimate=pl.CostEstimate(flops=1000000 * cells, bytes_accessed=0 * cells, transcendentals=6 * cells),
    )(jnp.concatenate([view_flag, slab_rank]), level_set, velocity)
    picture = jax.ShapeDtypeStruct((4, cols // slabs, rows), f32)
    first, second, field = pl.pallas_call(
        finish,
        out_shape=(picture, picture, level),
        in_specs=[near, near, pl.BlockSpec(memory_space=pl.ANY)],
        out_specs=(far, far, far),
        scratch_shapes=[pltpu.VMEM((2, 4, cols // slabs, rows), f32), dma((4,)), dma((2,))],
        compiler_params=pltpu.CompilerParams(vmem_limit_bytes=4 * 1024 * 1024),
        cost_estimate=pl.CostEstimate(flops=cells, bytes_accessed=8 * cells, transcendentals=0),
    )(*parts)
    return (first.transpose(0, 2, 1), second.transpose(0, 2, 1), field)


def solution(mesh):
    slabs, images = mesh.shape["depth"], mesh.shape["image"]

    def whole(level_set, velocity, view_flag, slab_rank):
        layers, rows, cols = level_set.shape
        dims = (slabs, images, layers // slabs, rows // images, cols)
        placed = (P("depth", "image", None), P(None, "depth", "image", None), P(), P())
        return jax.shard_map(
            functools.partial(local, dims),
            mesh=mesh,
            in_specs=placed,
            out_specs=(P(None, "image", "depth"), P(None, "image", "depth"), P("depth", "image", None)),
            check_vma=False,
        )(level_set, velocity, view_flag, slab_rank)

    return whole
```

time: 55.3 us -> 47.7 us (0.86)
  Pallas kernels: 53.8 us -> 46.2 us
    pallas_call x1, Pallas kernels: 51.8 us -> 44.8 us  [local(): pl.pallas_call(functools.partial(kernel, dims), out_shape=(packed, packed...]
    pallas_call x1, Pallas kernels: 1.98 us -> 1.39 us  [local(): pl.pallas_call(finish, out_shape=(picture, picture, level), in_specs=[nea...]
where the time goes in v2:
time: 47.7 us; the launch traced here: 47.6 us
  Pallas kernels  46.2 us (97%)
  other arithmetic  0.75 us (2%)
  between operations  0.64 us (1%)
    pallas_call x1, Pallas kernels, local(): pl.pallas_call(functools.partial(kernel, dims), out_shape=(packed, packed...  44.8 us
    pallas_call x1, Pallas kernels, local(): pl.pallas_call(finish, out_shape=(picture, picture, level), in_specs=[nea...  1.39 us

profile of v2, /device:TPU:1, one launch (start us, length us, event | category | flops | bytes accessed | tf_op | source)
XLA Modules:
  0.0 47.6 jit_solution(1494903181573235773)
XLA Ops:
  0.6 0.7 %pad_add_fusion.plan_hbm = s32[32]{0:T(128)S(1)} fusion(s32[16]{0:T(128)} %param.7, s32[16]{0:T(128)} %param.6), kind=kLoop, calls=%fused_computation | loop fusion | flops 32 | bytes 256 | tf_op jit(solution)/shard_map/concatenate | solution.py:409
  1.4 44.8 %shard_map.67 = (f32[4,16,128]{2,1,0:T(8,128)S(1)}, f32[4,16,128]{2,1,0:T(8,128)S(1)}, f32[16,64,512]{2,1,0:T(8,128)S(1)}) custom-call(s32[32]{0:T(128)S(1)} %pad_add_fusion.plan_hbm, f32[16,64,512]{2,1,0:T(8,128)} %field_hbm.1, f32[3,16,64,512]{3,2,1,0:T(8,128)} %speed_hbm.1), custom_call_target="tpu_custom_call" | custom-call | flops 524288000000 | tf_op jit(solution)/shard_map/pallas_call | solution.py:383
  46.2 1.4 %shard_map.68 = (f32[4,32,64]{2,1,0:T(8,128)}, f32[4,32,64]{2,1,0:T(8,128)}, f32[16,64,512]{2,1,0:T(8,128)}) custom-call(f32[4,16,128]{2,1,0:T(8,128)S(1)} %get-tuple-element.9.image_a, f32[4,16,128]{2,1,0:T(8,128)S(1)} %get-tuple-element.10.image_b, f32[16,64,512]{2,1,0:T(8,128)S(1)} %get-tuple-element.11.field), custom_call_target="tpu_custom_call" | custom-call | flops 524288 | bytes 4194304 | tf_op jit(solution)/shard_map/pallas_call | solution.py:411

commit v3 on v2

--- a/solution.py
+++ b/solution.py
@@ -100,7 +100,7 @@
         return jnp.where(lax.rem(n, 2) == 0, n // 2 + 1, slabs - (n + 1) // 2)
 
     def send(f, ch, n):
-        k = hop(n)
+        k = hop(slabs - 2 - n)
         to = lax.rem(d + k, slabs)
         pltpu.make_async_remote_copy(pk.at[f, to, ch], rc[f].at[d, ch], ss.at[f, ch, k], rs.at[f, ch, k],
                                      device_id={"depth": to}, device_id_type=MESH).start()
@@ -206,6 +206,22 @@
                     keep_rows(s + 1, slot(z, "inner"), low, 1)
                     keep_rows(s + 1, slot(z, "inner"), high, 0)
 
+    def edges(s, z, kind, t):
+        x_lo = (lambda c: xh[0, s, slot(z, kind), :, c]) if t == 0 else None
+        x_hi = (lambda c: xh[1, s, slot(z, kind), :, c]) if t == tiles - 1 else None
+        z_lo, z_hi = neighbours(s, z, kind)
+        advance(s, z, t, z_lo, z_hi, x_lo, x_hi)
+
+    def last_rows(s, ch):
+        @pl.loop(0, 2)
+        def _(half):
+            for q in range(inner // 2):
+                edges(s, 1 + half * (inner // 2) + q, "inner", ch * (tiles - 1))
+
+        for z, kind in ((0, "first"), (layers - 1, "last")):
+            for t in range(ch, tiles, CHUNKS):
+                edges(s, z, kind, t)
+
     def interior(s):
         @pl.loop(1, layers - 1)
         def _(z):
@@ -282,8 +298,7 @@
 
     keep_first(0, "first")
     keep_first(layers - 1, "last")
-    for ch in range(CHUNKS):
-        render(0, 0, ch)
+    render(0, 0, 0)
 
     pl.semaphore_wait(barrier, slabs + 1)
     for part in range(3):
@@ -299,6 +314,8 @@
         order[r] = found
     load_speed.wait()
     interior(0)
+    for ch in range(1, CHUNKS):
+        render(0, 0, ch)
     for s in range(STEPS - 1):
         for part in range(2):
             wait_x(s, part)
@@ -316,22 +333,25 @@
         interior(s + 1)
 
     last = STEPS - 1
-    for part in range(2):
+    for part in range(3):
         wait_x(last, part)
-        sides(last, part, False)
-    wait_x(last, 2)
-    wait_z(last, 0)
-    layer(last, 0, "first", False)
-    wait_z(last, 1)
-    layer(last, layers - 1, "last", False)
+    for side in range(2):
+        wait_z(last, side)
     for ch in range(CHUNKS):
+        last_rows(last, ch)
         render(STEPS, 1, ch)
         send_chunk(1, ch)
-    for f, image in ((0, image_a), (1, image_b)):
+
+    def wait_sends(f):
         for ch in range(CHUNKS):
-            wait_chunk(f, ch)
-        for ch in range(CHUNKS):
-            composite(f, ch, image)
+            @pl.loop(1, slabs)
+            def _(k):
+                chunk_copy(f, ch, k).wait_send()
+
+    for ch in range(CHUNKS):
+        wait_chunk(0, ch)
+    for ch in range(CHUNKS):
+        composite(0, ch, image_a)
 
     for side in range(2):
         @pl.when(d != (0 if side else slabs - 1))
@@ -345,12 +365,12 @@
                 for part in range(3):
                     x_copy(s, part, side).wait_send()
 
-    @pl.loop(0, CHUNKS)
-    def _(ch):
-        for f in range(2):
-            @pl.loop(1, slabs)
-            def _(k):
-                chunk_copy(f, ch, k).wait_send()
+    wait_sends(0)
+    wait_sends(1)
+    for ch in range(CHUNKS):
+        wait_chunk(1, ch)
+    for ch in range(CHUNKS):
+        composite(1, ch, image_b)
 
 
 def finish(image_a, image_b, field, first, second, next_hbm, picture, sem, out_sem):

time: 47.7 us -> 46 us (0.964)
  Pallas kernels: 46.2 us -> 44.5 us
    pallas_call x1, Pallas kernels: 44.8 us -> 43.1 us  [local(): pl.pallas_call(functools.partial(kernel, dims), out_shape=(packed, packed...]
where the time goes in v3:
time: 46 us; the launch traced here: 45.9 us
  Pallas kernels  44.5 us (97%)
  other arithmetic  0.75 us (2%)
  between operations  0.64 us (1%)
    pallas_call x1, Pallas kernels, local(): pl.pallas_call(functools.partial(kernel, dims), out_shape=(packed, packed...  43.1 us
    pallas_call x1, Pallas kernels, local(): pl.pallas_call(finish, out_shape=(picture, picture, level), in_specs=[nea...  1.39 us

profile of v3, /device:TPU:1, one launch (start us, length us, event | category | flops | bytes accessed | tf_op | source)
XLA Modules:
  0.0 45.9 jit_solution(804600527880958739)
XLA Ops:
  0.6 0.7 %pad_add_fusion.plan_hbm = s32[32]{0:T(128)S(1)} fusion(s32[16]{0:T(128)} %param.7, s32[16]{0:T(128)} %param.6), kind=kLoop, calls=%fused_computation | loop fusion | flops 32 | bytes 256 | tf_op jit(solution)/shard_map/concatenate | solution.py:429
  1.4 43.1 %shard_map.67 = (f32[4,16,128]{2,1,0:T(8,128)S(1)}, f32[4,16,128]{2,1,0:T(8,128)S(1)}, f32[16,64,512]{2,1,0:T(8,128)S(1)}) custom-call(s32[32]{0:T(128)S(1)} %pad_add_fusion.plan_hbm, f32[16,64,512]{2,1,0:T(8,128)} %field_hbm.1, f32[3,16,64,512]{3,2,1,0:T(8,128)} %speed_hbm.1), custom_call_target="tpu_custom_call" | custom-call | flops 524288000000 | tf_op jit(solution)/shard_map/pallas_call | solution.py:403
  44.5 1.4 %shard_map.68 = (f32[4,32,64]{2,1,0:T(8,128)}, f32[4,32,64]{2,1,0:T(8,128)}, f32[16,64,512]{2,1,0:T(8,128)}) custom-call(f32[4,16,128]{2,1,0:T(8,128)S(1)} %get-tuple-element.9.image_a, f32[4,16,128]{2,1,0:T(8,128)S(1)} %get-tuple-element.10.image_b, f32[16,64,512]{2,1,0:T(8,128)S(1)} %get-tuple-element.11.field), custom_call_target="tpu_custom_call" | custom-call | flops 524288 | bytes 4194304 | tf_op jit(solution)/shard_map/pallas_call | solution.py:431

commit v4 on v3

--- a/solution.py
+++ b/solution.py
@@ -57,7 +57,7 @@
     def slot(z, kind):
         return {"first": inner, "last": inner + 1}.get(kind, z - 1)
 
-    spans = ((0, inner // 2 + 1), (inner // 2 + 1, inner // 2 - 1), (inner, 2))
+    spans = ((0, inner), (inner, 2))
 
     def x_copy(s, part, side):
         where = pl.ds(*spans[part])
@@ -301,7 +301,7 @@
     render(0, 0, 0)
 
     pl.semaphore_wait(barrier, slabs + 1)
-    for part in range(3):
+    for part in range(2):
         start_x(0, part)
     for side in range(2):
         start_z(0, side)
@@ -317,23 +317,22 @@
     for ch in range(1, CHUNKS):
         render(0, 0, ch)
     for s in range(STEPS - 1):
-        for part in range(2):
-            wait_x(s, part)
-            sides(s, part, True)
-            start_x(s + 1, part)
-        wait_x(s, 2)
+        wait_x(s, 0)
+        sides(s, 0, True)
+        start_x(s + 1, 0)
+        wait_x(s, 1)
         wait_z(s, 0)
         layer(s, 0, "first", True)
         start_z(s + 1, 1)
         wait_z(s, 1)
         layer(s, layers - 1, "last", True)
         start_z(s + 1, 0)
-        start_x(s + 1, 2)
+        start_x(s + 1, 1)
         send_half(0, (s + 1) // 2, (s + 1) % 2)
         interior(s + 1)
 
     last = STEPS - 1
-    for part in range(3):
+    for part in range(2):
         wait_x(last, part)
     for side in range(2):
         wait_z(last, side)
@@ -362,7 +361,7 @@
         @pl.when(i != (0 if side else images - 1))
         def _():
             for s in range(STEPS):
-                for part in range(3):
+                for part in range(2):
                     x_copy(s, part, side).wait_send()
 
     wait_sends(0)
@@ -418,8 +417,8 @@
             dma((3,)),
             dma((2, STEPS)),
             dma((2, STEPS)),
-            dma((3, 2, STEPS)),
-            dma((3, 2, STEPS)),
+            dma((2, 2, STEPS)),
+            dma((2, 2, STEPS)),
             dma((2, CHUNKS, slabs)),
             dma((2, CHUNKS, slabs)),
             dma((2, CHUNKS)),

time: 46 us -> 45.2 us (0.983)
  Pallas kernels: 44.5 us -> 43.8 us
    pallas_call x1, Pallas kernels: 43.1 us -> 42.4 us  [local(): pl.pallas_call(functools.partial(kernel, dims), out_shape=(packed, packed...]
where the time goes in v4:
time: 45.2 us
  Pallas kernels  43.8 us (97%)
  other arithmetic  0.75 us (2%)
  between operations  0.64 us (1%)
    pallas_call x1, Pallas kernels, local(): pl.pallas_call(functools.partial(kernel, dims), out_shape=(packed, packed...  42.4 us
    pallas_call x1, Pallas kernels, local(): pl.pallas_call(finish, out_shape=(picture, picture, level), in_specs=[nea...  1.39 us

profile of v4, /device:TPU:1, one launch (start us, length us, event | category | flops | bytes accessed | tf_op | source)
XLA Modules:
  0.0 45.2 jit_solution(13046545063481413981)
XLA Ops:
  0.6 0.7 %pad_add_fusion.plan_hbm = s32[32]{0:T(128)S(1)} fusion(s32[16]{0:T(128)} %param.7, s32[16]{0:T(128)} %param.6), kind=kLoop, calls=%fused_computation | loop fusion | flops 32 | bytes 256 | tf_op jit(solution)/shard_map/concatenate | solution.py:428
  1.4 42.4 %shard_map.67 = (f32[4,16,128]{2,1,0:T(8,128)S(1)}, f32[4,16,128]{2,1,0:T(8,128)S(1)}, f32[16,64,512]{2,1,0:T(8,128)S(1)}) custom-call(s32[32]{0:T(128)S(1)} %pad_add_fusion.plan_hbm, f32[16,64,512]{2,1,0:T(8,128)} %field_hbm.1, f32[3,16,64,512]{3,2,1,0:T(8,128)} %speed_hbm.1), custom_call_target="tpu_custom_call" | custom-call | flops 524288000000 | tf_op jit(solution)/shard_map/pallas_call | solution.py:402
  43.8 1.4 %shard_map.68 = (f32[4,32,64]{2,1,0:T(8,128)}, f32[4,32,64]{2,1,0:T(8,128)}, f32[16,64,512]{2,1,0:T(8,128)}) custom-call(f32[4,16,128]{2,1,0:T(8,128)S(1)} %get-tuple-element.9.image_a, f32[4,16,128]{2,1,0:T(8,128)S(1)} %get-tuple-element.10.image_b, f32[16,64,512]{2,1,0:T(8,128)S(1)} %get-tuple-element.11.field), custom_call_target="tpu_custom_call" | custom-call | flops 524288 | bytes 4194304 | tf_op jit(solution)/shard_map/pallas_call | solution.py:430
